TPU v7x, 128 devices: a whole 4x4x4 slice. The times are simulated.
128 devices in a mesh: lat: 16 (over y_hi, x, core), lon: 8 (over y_lo, z).
Axes of the slice: x: 4, y: 4 (y_hi: 2, y_lo: 2; y = y_hi * 2 + y_lo), z: 4, core: 2. Of those that a mesh axis runs over, the one named last changes fastest.
Arguments:
- ensemble: float32 [2, 1, 2048, 16384], P(None, None, 'lat', 'lon'), may hold values from -6 to 6
- cross_mix: float32 [2, 2048, 16384], P(None, 'lat', 'lon'), may hold values from -0.5 to 0.5
- sea_mask: int32 [2048, 16384], P('lat', 'lon'), may hold values 0 or 1
- level_rates: float32 [2, 2], replicated, may hold values from 1 to 256, as said below
- panel_inverse: float32 [2, 2, 128, 128], replicated, may hold values from 0 to 1, as said below
- reduced_lon: float32 [2, 256, 256], replicated, as said below
- reduced_lat: float32 [2, 32, 32], replicated, as said below
Outputs:
- smoothed: float32 [2, 1, 2048, 16384], P(None, None, 'lat', 'lon')
Inputs may be any that keep to these rules, and one draw needn't show every extreme that they name: `level_rates`: the same for every point of a level. `panel_inverse`: the inverse of the 128 x 128 tridiagonal matrix whose diagonal entries are one plus twice a (that is 1 + 2*a) and whose entries beside the diagonal are -a, a taken from level_rates. `reduced_lon`: the inverse of the system that the longitude line solve's panel end values satisfy, for the given panel inverses and rates. `reduced_lat`: the inverse of the system that the latitude line solve's panel end values satisfy, for the given panel inverses and rates.
All inputs are finite; a program needn't handle non-finite values. No bound on the sum of `sea_mask` on one device may be relied on, other than what follows from the above.
Results may differ from a plain program's by a relative error of at most 0.00018.
Values sent between devices are 32-bit elements; how exact they have to be, the bound alone decides.
No kernel may reach another device: no remote copies, remote signals or barrier semaphores. Data moves between devices by JAX's collectives and lax.ppermute only.
A program may use at most 128 MiB of HBM per device.

v0:
```python
import jax
import jax.numpy as jnp
from jax import lax
from jax.sharding import PartitionSpec as P

STEPS = 2
highest = lax.Precision.HIGHEST


def with_halo(shard, sides, width, wrap):
    for axis, dim in sides:
        size, length = (lax.axis_size(axis), shard.shape[dim])
        up = [(i, (i + 1) % size) for i in range(size if wrap else size - 1)]
        down = [(j, i) for i, j in up]
        last = lax.slice_in_dim(shard, length - width, length, axis=dim)
        first = lax.slice_in_dim(shard, 0, width, axis=dim)
        before = lax.ppermute(last, axis, up)
        after = lax.ppermute(first, axis, down)
        shard = jnp.concatenate([before, shard, after], axis=dim)
    return shard


def cross_term(extended):
    return (
        extended[:, :, 2:, 2:]
        - extended[:, :, 2:, :-2]
        - extended[:, :, :-2, 2:]
        + extended[:, :, :-2, :-2]
    )


def explicit_terms(extended):
    centre = extended[:, :, 1:-1, 1:-1]
    along_lon = extended[:, :, 1:-1, 2:] - 2.0 * centre + extended[:, :, 1:-1, :-2]
    along_lat = extended[:, :, 2:, 1:-1] - 2.0 * centre + extended[:, :, :-2, 1:-1]
    return (along_lon, along_lat, cross_term(extended))


def lon_panels(values, inverse):
    panel = inverse.shape[1]
    dims = values.shape
    split = values.reshape(dims[:3] + (dims[3] // panel, panel))
    return jnp.einsum("lsrcq,lpq->lsrcp", split, inverse, precision=highest)


def lon_ends(solved):
    paired = jnp.stack((solved[..., 0], solved[..., -1]), axis=-1)
    return paired.reshape(paired.shape[:3] + (-1,))


def lon_finish(solved, prev_last, next_first, inverse, rate_lon):
    left_col = inverse[:, None, None, None, :, 0]
    right_col = inverse[:, None, None, None, :, -1]
    scale = rate_lon[:, None, None, None, None]
    result = solved + scale * (prev_last[..., None] * left_col + next_first[..., None] * right_col)
    return result.reshape(result.shape[:3] + (-1,))


def lon_solve(values, inverse, reduced, rate_lon):
    solved = lon_panels(values, inverse)
    bounds = jnp.einsum("lsrk,lmk->lsrm", lon_ends(solved), reduced, precision=highest)
    pairs = bounds.reshape(bounds.shape[:3] + (-1, 2))
    prev_last = jnp.roll(pairs[..., 1], 1, axis=-1)
    next_first = jnp.roll(pairs[..., 0], -1, axis=-1)
    return lon_finish(solved, prev_last, next_first, inverse, rate_lon)


def lat_panels(values, inverse):
    panel = inverse.shape[1]
    dims = values.shape
    split = values.reshape((dims[0], dims[1], dims[2] // panel, panel, dims[3]))
    return jnp.einsum("lscqw,lpq->lscpw", split, inverse, precision=highest)


def lat_ends(solved):
    paired = jnp.stack((solved[:, :, :, 0, :], solved[:, :, :, -1, :]), axis=3)
    return paired.reshape((paired.shape[0], paired.shape[1], -1, paired.shape[4]))


def lat_shifted(pairs):
    first_end = pairs[:, :, :, 0, :]
    last_end = pairs[:, :, :, 1, :]
    zero_row = jnp.zeros_like(last_end[:, :, :1])
    prev_last = jnp.concatenate((zero_row, last_end[:, :, :-1]), axis=2)
    next_first = jnp.concatenate((first_end[:, :, 1:], zero_row), axis=2)
    return (prev_last, next_first)


def lat_finish(solved, prev_last, next_first, inverse, rate_lat):
    left_col = inverse[:, None, None, :, 0][..., None]
    right_col = inverse[:, None, None, :, -1][..., None]
    scale = rate_lat[:, None, None, None, None]
    result = solved + scale * (
        prev_last[:, :, :, None, :] * left_col + next_first[:, :, :, None, :] * right_col
    )
    dims = result.shape
    return result.reshape((dims[0], dims[1], dims[2] * dims[3], dims[4]))


def lat_solve(values, inverse, reduced, rate_lat):
    solved = lat_panels(values, inverse)
    bounds = jnp.einsum("lskw,lmk->lsmw", lat_ends(solved), reduced, precision=highest)
    dims = bounds.shape
    pairs = bounds.reshape((dims[0], dims[1], -1, 2, dims[3]))
    prev_last, next_first = lat_shifted(pairs)
    return lat_finish(solved, prev_last, next_first, inverse, rate_lat)


def extend_block(values):
    wide = with_halo(values, (("lon", 3),), 1, True)
    return with_halo(wide, (("lat", 2),), 1, False)


def lon_lines_solve(values, inverse, reduced, rate_lon):
    finished = lon_solve(
        lax.all_to_all(values, "lon", split_axis=2, concat_axis=3, tiled=True),
        inverse,
        reduced,
        rate_lon,
    )
    return lax.all_to_all(finished, "lon", split_axis=3, concat_axis=2, tiled=True)


def lat_lines_solve(values, inverse, reduced, rate_lat):
    finished = lat_solve(
        lax.all_to_all(values, "lat", split_axis=3, concat_axis=2, tiled=True),
        inverse,
        reduced,
        rate_lat,
    )
    return lax.all_to_all(finished, "lat", split_axis=2, concat_axis=3, tiled=True)


def shards(ensemble, cross_mix, sea_mask, level_rates, panel_inverse, reduced_lon, reduced_lat):
    sea_float = sea_mask.astype(jnp.float32)[None, None]
    mixing = cross_mix[:, None]
    rate_lon = level_rates[0]
    rate_lat = level_rates[1]
    scale_lon = rate_lon[:, None, None, None]
    scale_lat = rate_lat[:, None, None, None]
    inverse_lon = panel_inverse[0]
    inverse_lat = panel_inverse[1]

    def solve_lon(values):
        return lon_lines_solve(values, inverse_lon, reduced_lon, rate_lon)

    def solve_lat(values):
        return lat_lines_solve(values, inverse_lat, reduced_lat, rate_lat)

    current = ensemble
    for repeat in range(STEPS):
        along_lon, along_lat, diagonal_diff = explicit_terms(extend_block(current))
        start_value = sea_float * (
            current
            + mixing * diagonal_diff
            + 2.0 * scale_lon * along_lon
            + 2.0 * scale_lat * along_lat
        )
        first_lon = solve_lon(start_value - scale_lon * along_lon)
        first_lat = solve_lat(first_lon - scale_lat * along_lat)
        correction = cross_term(extend_block(first_lat - current))
        corrected = start_value + 0.5 * mixing * correction
        second_lon = solve_lon(corrected - scale_lon * along_lon)
        second_lat = solve_lat(second_lon - scale_lat * along_lat)
        current = sea_float * second_lat
    return current


def solution(mesh):
    in_specs = (
        P(None, None, "lat", "lon"),
        P(None, "lat", "lon"),
        P("lat", "lon"),
        P(),
        P(),
        P(),
        P(),
    )
    out_specs = P(None, None, "lat", "lon")
    return jax.shard_map(shards, mesh=mesh, in_specs=in_specs, out_specs=out_specs, check_vma=False)
```

profile of v0, /device:TPU:1, one launch (start us, length us, event | category | flops | bytes accessed | tf_op | source)
XLA Modules:
  0.0 1259.1 jit_solution(113004368854663224)
XLA Ops:
  45.1 26.1 %all-to-all-done = f32[2,1,128,2048]{3,0,1,2:T(2,128)} async-done(((f32[2,1,128,2048]{3,0,1,2:T(2,128)}), f32[2,1,128,2048]{3,0,1,2:T(2,128)}, u32[]{:S(2)}, u32[]{:S(2)}) %all-to-all-start) | async-done | bytes 2097184 | tf_op jit(solution)/shard_map/all_to_all | solution.py:116
  103.6 24.7 %reshape.408 = f32[8,1,65536]{2,1,0:T(1,128)} reshape(f32[16384,1,2,16]{3,2,1,0:T(2,128)} %bitcast.331) | data formatting | bytes 4194304
  128.4 30.0 %all_to_all.264 = f32[8,1,65536]{2,1,0:T(1,128)} all-to-all(f32[8,1,65536]{2,1,0:T(1,128)} %reshape.408), channel_id=1, replica_groups=mesh['lat'=16,'lon'=8] {'lon'}, dimensions={0} | all-to-all | bytes 4194304 | tf_op jit(solution)/shard_map/all_to_all | solution.py:121
  167.3 31.9 %reshape.409 = f32[16384,1,2,16]{3,2,1,0:T(2,128)} reshape(f32[8,65536]{1,0:T(8,128)} %reduce.8) | data formatting | bytes 4194304
  238.5 28.4 %all-to-all-done.2 = f32[2,1,128,2048]{2,0,1,3:T(2,128)} async-done(((f32[2,1,128,2048]{2,0,1,3:T(2,128)}), f32[2,1,128,2048]{2,0,1,3:T(2,128)}, u32[]{:S(2)}, u32[]{:S(2)}) %all-to-all-start.2) | async-done | bytes 2097184 | tf_op jit(solution)/shard_map/all_to_all | solution.py:126
  283.1 33.5 %all_to_all.265 = f32[2,1,2048,128]{3,0,1,2:T(2,128)S(1)} all-to-all(f32[2,1,2048,128]{3,0,1,2:T(2,128)S(1)} %copy.178), channel_id=1, replica_groups=mesh['lat'=16,'lon'=8] {'lat'}, dimensions={2} | all-to-all | bytes 4194304 | tf_op jit(solution)/shard_map/all_to_all | solution.py:131
  356.3 28.1 %all_to_all.266 = f32[2,1,128,2048]{3,0,1,2:T(2,128)S(1)} all-to-all(f32[2,1,128,2048]{3,0,1,2:T(2,128)S(1)} %copy.181), channel_id=1, replica_groups=mesh['lat'=16,'lon'=8] {'lon'}, dimensions={2} | all-to-all | bytes 4194304 | tf_op jit(solution)/shard_map/all_to_all | solution.py:116
  415.2 24.7 %reshape.410 = f32[8,1,65536]{2,1,0:T(1,128)} reshape(f32[16384,1,2,16]{3,2,1,0:T(2,128)} %bitcast.333) | data formatting | bytes 4194304
  439.9 28.7 %all_to_all.267 = f32[8,1,65536]{2,1,0:T(1,128)} all-to-all(f32[8,1,65536]{2,1,0:T(1,128)} %reshape.410), channel_id=1, replica_groups=mesh['lat'=16,'lon'=8] {'lon'}, dimensions={0} | all-to-all | bytes 4194304 | tf_op jit(solution)/shard_map/all_to_all | solution.py:121
  477.0 32.1 %reshape.411 = f32[16384,1,2,16]{3,2,1,0:T(2,128)} reshape(f32[8,65536]{1,0:T(8,128)} %reduce.9) | data formatting | bytes 4194304
  538.9 37.6 %all_to_all.268 = f32[2,1,128,2048]{2,0,1,3:T(2,128)} all-to-all(f32[2,1,128,2048]{2,0,1,3:T(2,128)} %copy.195), channel_id=1, replica_groups=mesh['lat'=16,'lon'=8] {'lat'}, dimensions={3} | all-to-all | bytes 4194304 | tf_op jit(solution)/shard_map/all_to_all | solution.py:126
  592.7 31.8 %all_to_all.269 = f32[2,1,2048,128]{3,0,1,2:T(2,128)S(1)} all-to-all(f32[2,1,2048,128]{3,0,1,2:T(2,128)S(1)} %copy.200), channel_id=1, replica_groups=mesh['lat'=16,'lon'=8] {'lat'}, dimensions={2} | all-to-all | bytes 4194304 | tf_op jit(solution)/shard_map/all_to_all | solution.py:131
  669.3 28.4 %all_to_all.270 = f32[2,1,128,2048]{3,0,1,2:T(2,128)S(1)} all-to-all(f32[2,1,128,2048]{3,0,1,2:T(2,128)S(1)} %copy.202), channel_id=1, replica_groups=mesh['lat'=16,'lon'=8] {'lon'}, dimensions={2} | all-to-all | bytes 4194304 | tf_op jit(solution)/shard_map/all_to_all | solution.py:116
  728.7 24.8 %reshape.412 = f32[8,1,65536]{2,1,0:T(1,128)} reshape(f32[16384,1,2,16]{3,2,1,0:T(2,128)} %bitcast.335) | data formatting | bytes 4194304
  753.4 29.0 %all_to_all.271 = f32[8,1,65536]{2,1,0:T(1,128)} all-to-all(f32[8,1,65536]{2,1,0:T(1,128)} %reshape.412), channel_id=1, replica_groups=mesh['lat'=16,'lon'=8] {'lon'}, dimensions={0} | all-to-all | bytes 4194304 | tf_op jit(solution)/shard_map/all_to_all | solution.py:121
  790.9 31.8 %reshape.413 = f32[16384,1,2,16]{3,2,1,0:T(2,128)} reshape(f32[8,65536]{1,0:T(8,128)} %reduce.10) | data formatting | bytes 4194304
  854.6 36.3 %all_to_all.272 = f32[2,1,128,2048]{2,0,1,3:T(2,128)} all-to-all(f32[2,1,128,2048]{2,0,1,3:T(2,128)} %copy.216), channel_id=1, replica_groups=mesh['lat'=16,'lon'=8] {'lat'}, dimensions={3} | all-to-all | bytes 4194304 | tf_op jit(solution)/shard_map/all_to_all | solution.py:126
  907.2 31.8 %all_to_all.273 = f32[2,1,2048,128]{3,0,1,2:T(2,128)S(1)} all-to-all(f32[2,1,2048,128]{3,0,1,2:T(2,128)S(1)} %copy.221), channel_id=1, replica_groups=mesh['lat'=16,'lon'=8] {'lat'}, dimensions={2} | all-to-all | bytes 4194304 | tf_op jit(solution)/shard_map/all_to_all | solution.py:131
  980.8 28.4 %all_to_all.274 = f32[2,1,128,2048]{3,0,1,2:T(2,128)S(1)} all-to-all(f32[2,1,128,2048]{3,0,1,2:T(2,128)S(1)} %copy.223), channel_id=1, replica_groups=mesh['lat'=16,'lon'=8] {'lon'}, dimensions={2} | all-to-all | bytes 4194304 | tf_op jit(solution)/shard_map/all_to_all | solution.py:116
  1040.1 24.7 %reshape.414 = f32[8,1,65536]{2,1,0:T(1,128)} reshape(f32[16384,1,2,16]{3,2,1,0:T(2,128)} %bitcast.337) | data formatting | bytes 4194304
  1064.8 29.0 %all_to_all.275 = f32[8,1,65536]{2,1,0:T(1,128)} all-to-all(f32[8,1,65536]{2,1,0:T(1,128)} %reshape.414), channel_id=1, replica_groups=mesh['lat'=16,'lon'=8] {'lon'}, dimensions={0} | all-to-all | bytes 4194304 | tf_op jit(solution)/shard_map/all_to_all | solution.py:121
  1102.2 31.9 %reshape.415 = f32[16384,1,2,16]{3,2,1,0:T(2,128)} reshape(f32[8,65536]{1,0:T(8,128)} %reduce.11) | data formatting | bytes 4194304
  1165.9 36.4 %all_to_all.276 = f32[2,1,128,2048]{2,0,1,3:T(2,128)} all-to-all(f32[2,1,128,2048]{2,0,1,3:T(2,128)} %copy.237), channel_id=1, replica_groups=mesh['lat'=16,'lon'=8] {'lat'}, dimensions={3} | all-to-all | bytes 4194304 | tf_op jit(solution)/shard_map/all_to_all | solution.py:126
  1218.5 31.8 %all_to_all.277 = f32[2,1,2048,128]{3,0,1,2:T(2,128)S(1)} all-to-all(f32[2,1,2048,128]{3,0,1,2:T(2,128)S(1)} %copy.242), channel_id=1, replica_groups=mesh['lat'=16,'lon'=8] {'lat'}, dimensions={2} | all-to-all | bytes 4194304 | tf_op jit(solution)/shard_map/all_to_all | solution.py:131
  (238 shorter events, 535.9 us)
Async XLA Ops:
  0.0 84.5 %copy-start = (f32[2,256,256]{2,1,0:T(8,128)S(1)}, f32[2,256,256]{2,1,0:T(8,128)}, u32[]{:S(2)}) copy-start(f32[2,256,256]{2,1,0:T(8,128)} %param.12) | copy-start | bytes 1572868
  1.1 7.8 collective-permute-start.1
  6.8 5.9 collective-permute-start
  7.6 15.5 %copy-start.12 = (f32[2,2]{1,0:T(2,128)S(1)}, f32[2,2]{1,0:T(2,128)}, u32[]{:S(2)}) copy-start(f32[2,2]{1,0:T(2,128)} %param.10) | copy-start | bytes 52
  15.7 7.4 copy-start.5
  15.7 8.7 copy-start.1
  15.8 8.7 collective-permute-start.2
  20.0 4.4 collective-permute-start.3
  39.8 5.0 copy-start.10
  39.8 31.3 %all-to-all-start = ((f32[2,1,128,2048]{3,0,1,2:T(2,128)}), f32[2,1,128,2048]{3,0,1,2:T(2,128)}, u32[]{:S(2)}, u32[]{:S(2)}) async-start(f32[2,1,128,2048]{3,0,1,2:T(2,128)} %copy.159), calls=%async_computation | async-start | bytes 4194304 | tf_op jit(solution)/shard_map/all_to_all | solution.py:116
  229.0 37.9 %all-to-all-start.2 = ((f32[2,1,128,2048]{2,0,1,3:T(2,128)}), f32[2,1,128,2048]{2,0,1,3:T(2,128)}, u32[]{:S(2)}, u32[]{:S(2)}) async-start(f32[2,1,128,2048]{2,0,1,3:T(2,128)} %copy.173), calls=%async_computation.2 | async-start | bytes 4194304 | tf_op jit(solution)/shard_map/all_to_all | solution.py:126
  271.0 3.7 copy-start.11
  325.8 3.9 collective-permute-start.5
  326.2 5.9 collective-permute-start.4
  337.1 6.4 collective-permute-start.6
  341.5 3.1 collective-permute-start.7
  633.0 4.1 collective-permute-start.9
  635.1 5.9 collective-permute-start.8
  646.1 6.3 collective-permute-start.10
  650.5 3.1 collective-permute-start.11
  948.4 3.9 collective-permute-start.13
  950.2 5.9 collective-permute-start.12
  961.2 6.3 collective-permute-start.14
  965.6 3.1 collective-permute-start.15
  (7 other events, 9.3 us)
where the time goes:
time: 1270 us; the launch traced here: 1260 us
  local copies, waits for them, and re-layouts  524 us (41%)
  blocking collectives  441 us (35%)
  other arithmetic  130 us (10%)
  waiting for transfers between devices  79.7 us (6%)
  starting transfers between devices  51.7 us (4%)
  matrix products  31.6 us (2%)
    unnamed x34, local copies, waits for them, and re-layouts  236 us
    all_to_all x4, blocking collectives, lat_lines_solve(): lax.all_to_all(finished, 'lat', split_axis=2, concat_axis=3, tiled=True)  129 us
    all_to_all x4, blocking collectives, lon_lines_solve(): lax.all_to_all(finished, 'lon', split_axis=3, concat_axis=2, tiled=True)  117 us
    all_to_all x3, blocking collectives, lat_lines_solve(): lax.all_to_all(values, 'lat', split_axis=3, concat_axis=2, tiled=True)  110 us
    all_to_all x5, local copies, waits for them, and re-layouts, lon_lines_solve(): lax.all_to_all(finished, 'lon', split_axis=3, concat_axis=2, tiled=True)  86.9 us
    all_to_all x3, blocking collectives, lon_lines_solve(): lax.all_to_all(values, 'lon', split_axis=2, concat_axis=3, tiled=True)  84.8 us
    reshape x4, local copies, waits for them, and re-layouts, lon_finish(): return result.reshape(result.shape[:3] + (-1,))  57.4 us
    all_to_all x4, other arithmetic, lon_lines_solve(): lax.all_to_all(finished, 'lon', split_axis=3, concat_axis=2, tiled=True)  33.9 us
  transfers between devices with their start and end apart: 18, of which 13 were waited for; matrix products, arithmetic and copies ran while one was open for 0% of the time, Pallas kernels for 0%

commit v1 on v0

--- a/solution.py
+++ b/solution.py
@@ -118,7 +118,16 @@
         reduced,
         rate_lon,
     )
-    return lax.all_to_all(finished, "lon", split_axis=3, concat_axis=2, tiled=True)
+    lift_the_tails = lambda inputs, axis_id: jnp.concatenate(
+        lax.all_to_all(
+            jnp.stack(jnp.split(inputs, lax.axis_size(axis_id), axis=3)),
+            axis_name=axis_id,
+            split_axis=0,
+            concat_axis=0,
+        ),
+        axis=2,
+    )
+    return lift_the_tails(finished, "lon")
 
 
 def lat_lines_solve(values, inverse, reduced, rate_lat):

time: 1270 us -> 907 us (0.71)
  local copies, waits for them, and re-layouts: 524 us -> 215 us
  other arithmetic: 130 us -> 82.3 us
    unnamed x34 -> x66, local copies, waits for them, and re-layouts: 236 us -> 42.1 us
    all_to_all x5 -> x0, local copies, waits for them, and re-layouts: 86.9 us -> none  [lon_lines_solve(): lax.all_to_all(finished, 'lon', split_axis=3, concat_axis=2, tiled=True)]
    reshape x4, local copies, waits for them, and re-layouts: 57.4 us -> 11 us  [lon_finish(): return result.reshape(result.shape[:3] + (-1,))]
    all_to_all x4 -> x0, other arithmetic: 33.9 us -> none  [lon_lines_solve(): lax.all_to_all(finished, 'lon', split_axis=3, concat_axis=2, tiled=True)]
  transfers between devices with their start and end apart: 18 -> 18, of which waited for: 13 -> 14; matrix products, arithmetic and copies ran while one was open for 0% -> 0% of each run, Pallas kernels for 0% -> 0%
where the time goes in v1:
time: 907 us; the launch traced here: 898 us
  blocking collectives  437 us (48%)
  local copies, waits for them, and re-layouts  215 us (24%)
  other arithmetic  82.3 us (9%)
  waiting for transfers between devices  79.3 us (9%)
  starting transfers between devices  51.2 us (6%)
  matrix products  31.6 us (3%)
    all_to_all x4, blocking collectives, lat_lines_solve(): lax.all_to_all(finished, 'lat', split_axis=2, concat_axis=3, tiled=True)  129 us
    all_to_all x4, blocking collectives, lon_lines_solve(): lax.all_to_all(jnp.stack(jnp.split(inputs, lax.axis_size(axis_id), axis=3...  118 us
    all_to_all x3, blocking collectives, lat_lines_solve(): lax.all_to_all(values, 'lat', split_axis=3, concat_axis=2, tiled=True)  105 us
    all_to_all x3, blocking collectives, lon_lines_solve(): lax.all_to_all(values, 'lon', split_axis=2, concat_axis=3, tiled=True)  84.8 us
    unnamed x66, local copies, waits for them, and re-layouts  42.1 us
    reshape x4, local copies, waits for them, and re-layouts, lat_finish(): return result.reshape((dims[0], dims[1], dims[2] * dims[3], dims[4]))  30.4 us
    all_to_all x1, waiting for transfers between devices, lat_lines_solve(): lax.all_to_all(values, 'lat', split_axis=3, concat_axis=2, tiled=True)  28.4 us
    sub x2, other arithmetic, shards(): first_lon = solve_lon(start_value - scale_lon * along_lon)  26.2 us
  transfers between devices with their start and end apart: 18, of which 14 were waited for; matrix products, arithmetic and copies ran while one was open for 0% of the time, Pallas kernels for 0%

profile of v1, /device:TPU:1, one launch (start us, length us, event | category | flops | bytes accessed | tf_op | source)
XLA Modules:
  0.0 898.4 jit_solution(9806654872759436931)
XLA Ops:
  25.8 12.5 %multiply_subtract_fusion.1 = (f32[2,1,128,2048]{3,2,0,1:T(8,128)S(1)}, f32[2,1,128,2048]{3,2,0,1:T(8,128)}, f32[2,1,128,2048]{3,2,0,1:T(8,128)}) fusion(f32[2]{0:T(128)S(1)} %get-tuple-element.65, f32[2,1,128,2048]{3,2,0,1:T(8,128)S(1)} %bitcast.446, f32[2,1,128,1]{3,2,0,1:T(8,128)S(1)} %collective-permute-done, ...), kind=kLoop, calls=%fused_computation.110 | loop fusion | flops 13631488 | bytes 15765560 | tf_op jit(solution)/shard_map/sub | solution.py:168
  46.1 26.0 %all-to-all-done = f32[2,1,128,2048]{3,0,1,2:T(2,128)} async-done(((f32[2,1,128,2048]{3,0,1,2:T(2,128)}), f32[2,1,128,2048]{3,0,1,2:T(2,128)}, u32[]{:S(2)}, u32[]{:S(2)}) %all-to-all-start) | async-done | bytes 2097184 | tf_op jit(solution)/shard_map/all_to_all | solution.py:116
  103.8 28.9 %all_to_all.212 = f32[8,2,1,16,2048]{4,3,1,2,0:T(8,128)S(1)} all-to-all(f32[8,2,1,16,2048]{4,3,1,2,0:T(8,128)S(1)} %fusion.92), channel_id=1, replica_groups=mesh['lat'=16,'lon'=8] {'lon'}, dimensions={0} | all-to-all | bytes 4194304 | tf_op jit(solution)/shard_map/all_to_all | solution.py:122
  140.1 9.3 %all-to-all-start.2 = ((f32[2,1,128,2048]{2,0,1,3:T(2,128)}), f32[2,1,128,2048]{2,0,1,3:T(2,128)}, u32[]{:S(2)}, u32[]{:S(2)}) async-start(f32[2,1,128,2048]{2,0,1,3:T(2,128)} %copy.199), calls=%async_computation.2 | async-start | bytes 4194304 | tf_op jit(solution)/shard_map/all_to_all | solution.py:135
  149.6 28.4 %all-to-all-done.2 = f32[2,1,128,2048]{2,0,1,3:T(2,128)} async-done(((f32[2,1,128,2048]{2,0,1,3:T(2,128)}), f32[2,1,128,2048]{2,0,1,3:T(2,128)}, u32[]{:S(2)}, u32[]{:S(2)}) %all-to-all-start.2) | async-done | bytes 2097184 | tf_op jit(solution)/shard_map/all_to_all | solution.py:135
  186.7 7.6 copy.204
  194.3 33.5 %all_to_all.213 = f32[2,1,2048,128]{3,0,1,2:T(2,128)S(1)} all-to-all(f32[2,1,2048,128]{3,0,1,2:T(2,128)S(1)} %copy.204), channel_id=1, replica_groups=mesh['lat'=16,'lon'=8] {'lat'}, dimensions={2} | all-to-all | bytes 4194304 | tf_op jit(solution)/shard_map/all_to_all | solution.py:140
  255.9 9.8 %fusion.37 = f32[2,1,128,2048]{3,2,0,1:T(8,128)S(1)} fusion(f32[2,1,128,2048]{3,2,0,1:T(8,128)} %get-tuple-element.12, f32[2,1,1,2050]{3,2,0,1:T(1,128)S(1)} %collective-permute-done.7, f32[2,1,128,2050]{3,2,0,1:T(8,128)} %concatenate.123, f32[2,1,1,2050]{3,2,0,1:T(1,128)S(1)} %collective-permute-done.6, f32[2,128,2048]{2,1,0:T(8,128)} %param.8, ...), kind=kLoop, calls=%fused_computation.61 | loop fusion | flops 8912896 | bytes 10522664 | tf_op jit(solution)/shard_map/sub | solution.py:172
  267.4 28.1 %all_to_all.214 = f32[2,1,128,2048]{3,0,1,2:T(2,128)S(1)} all-to-all(f32[2,1,128,2048]{3,0,1,2:T(2,128)S(1)} %copy.207), channel_id=1, replica_groups=mesh['lat'=16,'lon'=8] {'lon'}, dimensions={2} | all-to-all | bytes 4194304 | tf_op jit(solution)/shard_map/all_to_all | solution.py:116
  325.4 29.7 %all_to_all.215 = f32[8,2,1,16,2048]{4,3,1,2,0:T(8,128)S(1)} all-to-all(f32[8,2,1,16,2048]{4,3,1,2,0:T(8,128)S(1)} %fusion.84), channel_id=1, replica_groups=mesh['lat'=16,'lon'=8] {'lon'}, dimensions={0} | all-to-all | bytes 4194304 | tf_op jit(solution)/shard_map/all_to_all | solution.py:122
  362.5 35.1 %all_to_all.216 = f32[2,1,128,2048]{2,0,1,3:T(2,128)} all-to-all(f32[2,1,128,2048]{2,0,1,3:T(2,128)} %copy.219), channel_id=1, replica_groups=mesh['lat'=16,'lon'=8] {'lat'}, dimensions={3} | all-to-all | bytes 4194304 | tf_op jit(solution)/shard_map/all_to_all | solution.py:135
  406.2 7.6 copy.224
  413.8 31.9 %all_to_all.217 = f32[2,1,2048,128]{3,0,1,2:T(2,128)S(1)} all-to-all(f32[2,1,2048,128]{3,0,1,2:T(2,128)S(1)} %copy.224), channel_id=1, replica_groups=mesh['lat'=16,'lon'=8] {'lat'}, dimensions={2} | all-to-all | bytes 4194304 | tf_op jit(solution)/shard_map/all_to_all | solution.py:140
  474.4 13.8 %multiply_subtract_fusion = (f32[2,1,128,2048]{3,2,0,1:T(8,128)S(1)}, f32[2,1,128,2048]{3,2,0,1:T(8,128)}) fusion(f32[2]{0:T(128)S(1)} %get-tuple-element.65, f32[2,1,128,2048]{3,2,0,1:T(8,128)} %copy-done.6, f32[2,1,128,1]{3,2,0,1:T(8,128)S(1)} %collective-permute-done.8, f32[2,1,128,1]{3,2,0,1:T(8,128)S(1)} %collective-permute-done.9, ...), kind=kLoop, calls=%fused_computation.109 | loop fusion | flops 13107200 | bytes 11571256 | tf_op jit(solution)/shard_map/sub | solution.py:168
  489.8 28.4 %all_to_all.218 = f32[2,1,128,2048]{3,0,1,2:T(2,128)S(1)} all-to-all(f32[2,1,128,2048]{3,0,1,2:T(2,128)S(1)} %copy.226), channel_id=1, replica_groups=mesh['lat'=16,'lon'=8] {'lon'}, dimensions={2} | all-to-all | bytes 4194304 | tf_op jit(solution)/shard_map/all_to_all | solution.py:116
  548.1 30.0 %all_to_all.219 = f32[8,2,1,16,2048]{4,3,1,2,0:T(8,128)S(1)} all-to-all(f32[8,2,1,16,2048]{4,3,1,2,0:T(8,128)S(1)} %fusion.76), channel_id=1, replica_groups=mesh['lat'=16,'lon'=8] {'lon'}, dimensions={0} | all-to-all | bytes 4194304 | tf_op jit(solution)/shard_map/all_to_all | solution.py:122
  586.5 35.0 %all_to_all.220 = f32[2,1,128,2048]{2,0,1,3:T(2,128)} all-to-all(f32[2,1,128,2048]{2,0,1,3:T(2,128)} %copy.238), channel_id=1, replica_groups=mesh['lat'=16,'lon'=8] {'lat'}, dimensions={3} | all-to-all | bytes 4194304 | tf_op jit(solution)/shard_map/all_to_all | solution.py:135
  630.2 7.6 copy.243
  637.8 31.9 %all_to_all.221 = f32[2,1,2048,128]{3,0,1,2:T(2,128)S(1)} all-to-all(f32[2,1,2048,128]{3,0,1,2:T(2,128)S(1)} %copy.243), channel_id=1, replica_groups=mesh['lat'=16,'lon'=8] {'lat'}, dimensions={2} | all-to-all | bytes 4194304 | tf_op jit(solution)/shard_map/all_to_all | solution.py:140
  698.7 9.7 %fusion.29 = f32[2,1,128,2048]{3,2,0,1:T(8,128)S(1)} fusion(f32[2,1,128,2048]{3,2,0,1:T(8,128)} %get-tuple-element.10, f32[2,1,1,2050]{3,2,0,1:T(1,128)S(1)} %collective-permute-done.15, f32[2,1,128,2050]{3,2,0,1:T(8,128)} %concatenate.139, f32[2,1,1,2050]{3,2,0,1:T(1,128)S(1)} %collective-permute-done.14, f32[2,128,2048]{2,1,0:T(8,128)} %param.8, ...), kind=kLoop, calls=%fused_computation.53 | loop fusion | flops 8912896 | bytes 10522664 | tf_op jit(solution)/shard_map/sub | solution.py:172
  710.0 28.4 %all_to_all.222 = f32[2,1,128,2048]{3,0,1,2:T(2,128)S(1)} all-to-all(f32[2,1,128,2048]{3,0,1,2:T(2,128)S(1)} %copy.245), channel_id=1, replica_groups=mesh['lat'=16,'lon'=8] {'lon'}, dimensions={2} | all-to-all | bytes 4194304 | tf_op jit(solution)/shard_map/all_to_all | solution.py:116
  768.3 29.8 %all_to_all.223 = f32[8,2,1,16,2048]{4,3,1,2,0:T(8,128)S(1)} all-to-all(f32[8,2,1,16,2048]{4,3,1,2,0:T(8,128)S(1)} %fusion.68), channel_id=1, replica_groups=mesh['lat'=16,'lon'=8] {'lon'}, dimensions={0} | all-to-all | bytes 4194304 | tf_op jit(solution)/shard_map/all_to_all | solution.py:122
  806.6 35.0 %all_to_all.224 = f32[2,1,128,2048]{2,0,1,3:T(2,128)} all-to-all(f32[2,1,128,2048]{2,0,1,3:T(2,128)} %copy.257), channel_id=1, replica_groups=mesh['lat'=16,'lon'=8] {'lat'}, dimensions={3} | all-to-all | bytes 4194304 | tf_op jit(solution)/shard_map/all_to_all | solution.py:135
  857.8 31.9 %all_to_all.225 = f32[2,1,2048,128]{3,0,1,2:T(2,128)S(1)} all-to-all(f32[2,1,2048,128]{3,0,1,2:T(2,128)S(1)} %copy.262), channel_id=1, replica_groups=mesh['lat'=16,'lon'=8] {'lat'}, dimensions={2} | all-to-all | bytes 4194304 | tf_op jit(solution)/shard_map/all_to_all | solution.py:140
  (273 shorter events, 327.3 us)
Async XLA Ops:
  0.0 85.4 %copy-start = (f32[2,256,256]{2,1,0:T(8,128)S(1)}, f32[2,256,256]{2,1,0:T(8,128)}, u32[]{:S(2)}) copy-start(f32[2,256,256]{2,1,0:T(8,128)} %param.12) | copy-start | bytes 1572868
  1.1 7.8 collective-permute-start.1
  6.8 5.9 collective-permute-start
  7.6 17.4 %copy-start.18 = (f32[2,2]{1,0:T(2,128)S(1)}, f32[2,2]{1,0:T(2,128)}, u32[]{:S(2)}) copy-start(f32[2,2]{1,0:T(2,128)} %param.10) | copy-start | bytes 52
  7.6 17.4 %copy-start.16 = (s32[128,2048]{1,0:T(8,128)S(1)}, s32[128,2048]{1,0:T(8,128)}, u32[]{:S(2)}) copy-start(s32[128,2048]{1,0:T(8,128)} %param.9) | copy-start | bytes 3145732
  16.7 9.1 %copy-start.1 = (f32[2,1,128,2048]{3,2,1,0:T(8,128)S(1)}, f32[2,1,128,2048]{3,2,1,0:T(8,128)}, u32[]{:S(2)}) copy-start(f32[2,1,128,2048]{3,2,1,0:T(8,128)} %param.7) | copy-start | bytes 6291460
  17.9 7.2 collective-permute-start.2
  21.9 3.9 collective-permute-start.3
  41.2 30.9 %all-to-all-start = ((f32[2,1,128,2048]{3,0,1,2:T(2,128)}), f32[2,1,128,2048]{3,0,1,2:T(2,128)}, u32[]{:S(2)}, u32[]{:S(2)}) async-start(f32[2,1,128,2048]{3,0,1,2:T(2,128)} %copy.187), calls=%async_computation | async-start | bytes 4194304 | tf_op jit(solution)/shard_map/all_to_all | solution.py:116
  140.1 37.9 %all-to-all-start.2 = ((f32[2,1,128,2048]{2,0,1,3:T(2,128)}), f32[2,1,128,2048]{2,0,1,3:T(2,128)}, u32[]{:S(2)}, u32[]{:S(2)}) async-start(f32[2,1,128,2048]{2,0,1,3:T(2,128)} %copy.199), calls=%async_computation.2 | async-start | bytes 4194304 | tf_op jit(solution)/shard_map/all_to_all | solution.py:135
  237.1 3.9 collective-permute-start.5
  237.5 5.9 collective-permute-start.4
  248.4 6.8 collective-permute-start.6
  252.8 3.1 collective-permute-start.7
  454.2 3.9 collective-permute-start.9
  456.0 5.9 collective-permute-start.8
  466.9 6.5 collective-permute-start.10
  471.3 3.1 collective-permute-start.11
  548.1 30.2 %copy-start.4 = (f32[2,1,128,2050]{3,2,0,1:T(8,128)S(1)}, f32[2,1,128,2050]{3,2,0,1:T(8,128)}, u32[]{:S(2)}) copy-start(f32[2,1,128,2050]{3,2,0,1:T(8,128)} %concatenate.130) | copy-start | bytes 6297604
  679.0 3.9 collective-permute-start.13
  680.1 6.1 collective-permute-start.12
  691.2 6.3 collective-permute-start.14
  695.6 3.1 collective-permute-start.15
  768.3 30.0 %copy-start.5 = (f32[2,1,128,2050]{3,2,0,1:T(8,128)S(1)}, f32[2,1,128,2050]{3,2,0,1:T(8,128)}, u32[]{:S(2)}) copy-start(f32[2,1,128,2050]{3,2,0,1:T(8,128)} %concatenate.130) | copy-start | bytes 6297604
  (13 other events, 24.0 us)
